TPU v7x, 32 devices: a whole 2x2x4 slice. The times are simulated.
32 devices in a mesh: slab: 8 (over y, x, core), sub: 4 (over z).
Axes of the slice: x: 2, y: 2, z: 4, core: 2. Of those that a mesh axis runs over, the one named last changes fastest.
Arguments:
- cav_disp: float32 [3, 512, 128, 128], P(None, 'slab', 'sub'), may hold values from -2 to 2
- cav_load: float32 [3, 512, 128, 128], P(None, 'slab', 'sub'), may hold values from -6 to 6
- cav_stiff: float32 [512, 128, 128], P('slab', 'sub'), may hold values from 0.5 to 4
- cav_clamp: int32 [512, 128, 128], P('slab', 'sub'), may hold values 0 or 1
- mnt_disp: float32 [3, 512, 128, 128], P(None, 'slab', 'sub'), may hold values from -2 to 2
- mnt_load: float32 [3, 512, 128, 128], P(None, 'slab', 'sub'), may hold values from -6 to 6
- mnt_stiff: float32 [512, 128, 128], P('slab', 'sub'), may hold values from 0.5 to 4
- mnt_clamp: int32 [512, 128, 128], P('slab', 'sub'), may hold values 0 or 1
- pair_owner: int32 [65536, 1], P(('slab', 'sub')), may hold values from 0 to 31, as said below
- pair_row: int32 [65536], P(('slab', 'sub')), may hold values from 0 to 2047
- pair_seg: int32 [65536], P(('slab', 'sub')), may hold values from 0 to 2047
- pair_weight: float32 [65536], P(('slab', 'sub')), may hold values from 0.2 to 2
- pair_tilt: float32 [2, 65536], P(None, ('slab', 'sub')), may hold values from -0.5 to 0.5
- pair_gap: float32 [65536], P(('slab', 'sub')), may hold values from -3 to 3
Outputs:
- cav_new: float32 [3, 512, 128, 128], P(None, 'slab', 'sub')
- mnt_new: float32 [3, 512, 128, 128], P(None, 'slab', 'sub')
Inputs may be any that keep to these rules, and one draw needn't show every extreme that they name: `pair_owner`: the owner of a pair lies in the holder's slab or in the next slab along the long axis. Among the pairs of one device, at most 512 name one owner, and some owner is named exactly 512 times.
All inputs are finite; a program needn't handle non-finite values. No bound on the sum of `cav_clamp` or of `mnt_clamp` on one device may be relied on, other than what follows from the above.
Results may differ from a plain program's by a relative error of at most 0.00002.
Values sent between devices are 32-bit elements; how exact they have to be, the bound alone decides.
A program may use at most 128 MiB of HBM per device.

v0:
```python
import functools
import jax
import jax.numpy as jnp
from jax import lax
from jax.experimental import pallas as pl
from jax.experimental.pallas import tpu as pltpu
from jax.sharding import PartitionSpec as P

OMEGA = 0.8
KCLAMP = 4.0
KNORM = 2.0
BETA = 4.0
MESH = pl.DeviceIdType.MESH
F32 = jnp.float32
BF16 = jnp.bfloat16
CHUNK = 256


def split3(v):
    hi = v.astype(BF16).astype(F32)
    rest = v - hi
    mid = rest.astype(BF16).astype(F32)
    return hi, mid, rest - mid


def beside_z(v):
    axis = v.ndim - 1
    depth = v.shape[axis]
    lane = lax.broadcasted_iota(jnp.int32, v.shape, axis)
    up = jnp.where(lane == 0, 0.0, pltpu.roll(v, 1, axis))
    down = jnp.where(lane == depth - 1, 0.0, pltpu.roll(v, depth - 1, axis))
    return up + down


def beside_rows(v, before, after):
    rows = v.shape[0]
    at = lax.broadcasted_iota(jnp.int32, v.shape, 0)
    up = jnp.where(at == 0, before, pltpu.roll(v, 1, 0))
    down = jnp.where(at == rows - 1, after, pltpu.roll(v, rows - 1, 0))
    return up + down


def coefficients(stiff, clamp):
    gain = OMEGA / (6.0 * stiff + KCLAMP * clamp.astype(F32))
    return gain, gain * stiff


def contact_kernel(
    n_slab, n_sub, nx, ny,
    disp_c, disp_m, load_c, load_m, stiff_c, stiff_m, clamp_c, clamp_m,
    seg, row, own, weight, gap0, tilt,
    react, xh0, yh0, xh1, yh1,
    u, ld, st, cl, tab, part, rec, yf, xs1, ys1,
    tab_s, tab_r, part_s, part_r, h0_s, h0_r, h1_s, h1_r, in_sem,
):
    s = lax.axis_index("slab")
    t = lax.axis_index("sub")
    depth = 128
    cells = nx * ny
    half = ny // 2
    dense = 3 * half
    pairs = seg.shape[0] * 128
    has_prev = s > 0
    has_next = s < n_slab - 1
    lane_of = (depth - 1, 0)

    loads = []
    for i, (src, dst) in enumerate((
        (disp_m, u.at[1]), (disp_c, u.at[0]),
        (stiff_m, st.at[1]), (clamp_m, cl.at[1]), (load_m, ld.at[1]),
        (stiff_c, st.at[0]), (clamp_c, cl.at[0]), (load_c, ld.at[0]),
    )):
        copy = pltpu.make_async_copy(src, dst, in_sem.at[i])
        copy.start()
        loads.append(copy)

    def peer(ds, d):
        return {"slab": s + ds, "sub": lax.rem(t + d, n_sub)}

    barrier = pltpu.get_barrier_semaphore()
    for d in range(1, n_sub):
        pl.semaphore_signal(barrier, inc=1, device_id=peer(0, d), device_id_type=MESH)

    @pl.when(has_prev)
    def _():
        for d in range(n_sub):
            pl.semaphore_signal(barrier, inc=1, device_id=peer(-1, d), device_id_type=MESH)

    @pl.when(has_next)
    def _():
        for d in range(n_sub):
            pl.semaphore_signal(barrier, inc=1, device_id=peer(1, d), device_id_type=MESH)

    def densify(b):
        zc = lane_of[b]
        lane = lax.broadcasted_iota(jnp.int32, (half, depth), 1)

        def at_x(x, acc):
            acc = list(acc)
            for c in range(3):
                for h in range(2):
                    want = x + nx * h
                    start = pl.multiple_of(c * cells + x * ny + half * h, 8)
                    tile = u[b, pl.ds(start, half), :]
                    moved = pltpu.roll(tile, lax.rem(want - zc + depth, depth), 1)
                    acc[c] = jnp.where(lane == want, moved, acc[c])
            return tuple(acc)

        zero = jnp.zeros((half, depth), F32)
        return jnp.concatenate(lax.fori_loop(0, nx, at_x, (zero,) * 3, unroll=4), axis=0)

    loads[0].wait()
    tab[t] = densify(1)
    for b, side in ((1, 0), (1, 1)):
        for c in range(3):
            yf[b, side, c] = u[b, pl.ds(c * cells + side * (ny - 1), nx, stride=ny), :]

    sides = has_prev.astype(jnp.int32) + has_next.astype(jnp.int32)
    pl.semaphore_wait(barrier, n_sub - 1 + n_sub * sides)

    def remote(src, dst, ss, rs, dev):
        return pltpu.make_async_remote_copy(
            src_ref=src, dst_ref=dst, send_sem=ss, recv_sem=rs, device_id=dev, device_id_type=MESH
        )

    def tab_copy(ds, d):
        k = d if ds == 0 else n_sub + d
        slot = t if ds == 0 else n_sub + t
        return remote(tab.at[t], tab.at[slot], tab_s.at[k], tab_r.at[slot], peer(ds, d))

    def tab_arrival(ds, d):
        slot = lax.rem(t + d, n_sub) + (n_sub if ds else 0)
        return remote(tab.at[t], tab.at[slot], tab_s.at[0], tab_r.at[slot], peer(ds, d))

    for d in range(1, n_sub):
        tab_copy(0, d).start()

    @pl.when(has_prev)
    def _():
        for d in range(n_sub):
            tab_copy(-1, d).start()

    @pl.when(jnp.logical_not(has_next))
    def _():
        tab[pl.ds(n_sub, n_sub)] = jnp.zeros((n_sub, dense, depth), F32)

    def ways():
        return (
            (0, has_prev, {"slab": s - 1, "sub": t}),
            (1, has_next, {"slab": s + 1, "sub": t}),
            (2, t > 0, {"slab": s, "sub": t - 1}),
            (3, t < n_sub - 1, {"slab": s, "sub": t + 1}),
        )

    def halo_copy(b, way, dev, xsrc, ysrc, xdst, ydst, ss, rs):
        other = way ^ 1
        if way < 2:
            src, dst = xsrc(b, way), xdst.at[b, other]
        else:
            src, dst = ysrc.at[b, way - 2], ydst.at[b, other - 2]
        return remote(src, dst, ss.at[b, way], rs.at[b, other], dev)

    def halo_arrival(b, way, dev, xdst, ydst, ss, rs):
        dst = xdst.at[b, way] if way < 2 else ydst.at[b, way - 2]
        return remote(dst, dst, ss.at[b, way], rs.at[b, way], dev)

    def x_plane(b, way):
        return u.at[b].reshape(3, nx, ny, depth).at[:, (nx - 1) * way]

    def start_halo0(b):
        for way, there, dev in ways():
            @pl.when(there)
            def _():
                halo_copy(b, way, dev, x_plane, yf, xh0, yh0, h0_s, h0_r).start()

            @pl.when(jnp.logical_not(there))
            def _():
                for out_x, out_y in ((xh0, yh0), (xh1, yh1)):
                    if way < 2:
                        out_x[b, way] = jnp.zeros((3, ny, depth), F32)
                    else:
                        out_y[b, way - 2] = jnp.zeros((3, nx, depth), F32)

    start_halo0(1)
    loads[1].wait()
    for side in range(2):
        for c in range(3):
            yf[0, side, c] = u[0, pl.ds(c * cells + side * (ny - 1), nx, stride=ny), :]
    start_halo0(0)
    cav_dense = densify(0)
    cav_parts = jnp.concatenate([v.astype(BF16) for v in split3(cav_dense)], axis=1)

    for d in range(1, n_sub):
        tab_arrival(0, d).wait_recv()

    @pl.when(has_next)
    def _():
        for d in range(n_sub):
            tab_arrival(1, d).wait_recv()

    targets = 2 * n_sub
    table = tab[...].reshape(targets * dense, depth)
    tab_parts = jnp.concatenate([v.astype(BF16) for v in split3(table)], axis=1)

    def line(ref, k):
        per = CHUNK // 128
        return jnp.concatenate([ref[k * per + i : k * per + i + 1, :] for i in range(per)], axis=1)

    dot = functools.partial(
        lax.dot_general, preferred_element_type=F32, precision=lax.Precision.DEFAULT
    )
    mnt_sum = jnp.zeros((targets * dense, depth), F32)
    cav_sum = jnp.zeros((dense, depth), F32)
    lane_id = lax.broadcasted_iota(jnp.int32, (depth, CHUNK), 0)
    key_id = lax.broadcasted_iota(jnp.int32, (targets * half, CHUNK), 0)
    small_id = lax.broadcasted_iota(jnp.int32, (half, CHUNK), 0)
    for k in range(pairs // CHUNK):
        def lanes(cell):
            return cell // ny + nx * (cell % ny // half)

        seg_k, row_k = line(seg, k), line(row, k)
        target = line(own, k) - s * n_sub
        hot_m = (lane_id == lanes(seg_k)).astype(F32).astype(BF16)
        hot_c = (lane_id == lanes(row_k)).astype(F32).astype(BF16)
        mask_m = key_id == target * half + seg_k % half
        mask_c = small_id == row_k % half
        rows_m = dot(tab_parts, jnp.concatenate([hot_m] * 3, axis=0), (((1,), (0,)), ((), ())))
        rows_c = dot(cav_parts, jnp.concatenate([hot_c] * 3, axis=0), (((1,), (0,)), ((), ())))
        sl_a = tilt[0:1, k * CHUNK : (k + 1) * CHUNK]
        sl_b = tilt[1:2, k * CHUNK : (k + 1) * CHUNK]
        scale = 1.0 / jnp.sqrt(1.0 + sl_a * sl_a + sl_b * sl_b)
        normal = (sl_a * scale, sl_b * scale, scale)
        gap = line(gap0, k)
        for c in range(3):
            mine = jnp.concatenate(
                [rows_m[o * dense + c * half : o * dense + (c + 1) * half] for o in range(targets)], axis=0
            )
            side_m = jnp.sum(jnp.where(mask_m, mine, 0.0), axis=0, keepdims=True)
            side_c = jnp.sum(
                jnp.where(mask_c, rows_c[c * half : (c + 1) * half], 0.0), axis=0, keepdims=True
            )
            gap = gap + normal[c] * (side_c - side_m)
        z = -BETA * gap
        soft = jnp.maximum(z, 0.0) + jnp.log1p(jnp.exp(-jnp.abs(z)))
        press = line(weight, k) * (KNORM * soft / BETA)
        push = [split3(press * normal[c]) for c in range(3)]
        left_m, left_c = [], []
        for p in range(3):
            left_m.append(jnp.concatenate(
                [
                    jnp.where(mask_m[o * half : (o + 1) * half], push[c][p], 0.0)
                    for o in range(targets) for c in range(3)
                ], axis=0).astype(BF16))
            left_c.append(jnp.concatenate(
                [jnp.where(mask_c, push[c][p], 0.0) for c in range(3)], axis=0).astype(BF16))
        mnt_sum = mnt_sum + dot(
            jnp.concatenate(left_m, axis=1), jnp.concatenate([hot_m] * 3, axis=1), (((1,), (1,)), ((), ())))
        cav_sum = cav_sum + dot(
            jnp.concatenate(left_c, axis=1), jnp.concatenate([hot_c] * 3, axis=1), (((1,), (1,)), ((), ())))
    part[...] = mnt_sum.reshape(targets, dense, depth)
    react[0] = cav_sum

    def part_copy(ds, d):
        k = d if ds == 0 else n_sub + d
        slot = t if ds == 0 else n_sub + t
        block = lax.rem(t + d, n_sub) + (n_sub if ds else 0)
        return remote(part.at[block], rec.at[slot], part_s.at[k], part_r.at[slot], peer(ds, d))

    def part_arrival(ds, d):
        slot = lax.rem(t + d, n_sub) + (n_sub if ds else 0)
        return remote(part.at[t], rec.at[slot], part_s.at[0], part_r.at[slot], peer(ds, d))

    @pl.when(has_next)
    def _():
        for d in range(n_sub):
            part_copy(1, d).start()

    for d in range(1, n_sub):
        part_copy(0, d).start()
    rec[t] = part[t]

    @pl.when(jnp.logical_not(has_prev))
    def _():
        rec[pl.ds(n_sub, n_sub)] = jnp.zeros((n_sub, dense, depth), F32)

    for copy in loads[2:]:
        copy.wait()
    for b in range(2):
        for way, there, dev in ways():
            @pl.when(there)
            def _():
                halo_arrival(b, way, dev, xh0, yh0, h0_s, h0_r).wait_recv()

    def faces(b):
        zc = lane_of[b]
        force_b = react[b]
        turned = jnp.transpose(jnp.concatenate(
            [force_b, jnp.zeros((depth - dense, depth), F32)], axis=0))
        for side in range(2):
            x0 = side * (nx - 1)
            at_x = pl.ds(x0 * ny, ny)
            gain, pull = coefficients(st[b, at_x, :], cl[b, at_x, :])
            lane = lax.broadcasted_iota(jnp.int32, (ny, depth), 1)
            for c in range(3):
                v = u[b, pl.ds(c * cells + x0 * ny, ny), :]
                inner = u[b, pl.ds(c * cells + (x0 + 1 - 2 * side) * ny, ny), :]
                near = xh0[b, side, c] + inner + beside_z(v)
                near = near + beside_rows(v, yh0[b, 0, c, x0 : x0 + 1], yh0[b, 1, c, x0 : x0 + 1])
                rows = force_b[c * half : (c + 1) * half]
                extra = jnp.concatenate(
                    [pltpu.roll(rows, (zc - x0 - nx * h) % depth, 1) for h in range(2)], axis=0)
                force = ld[b, pl.ds(c * cells + x0 * ny, ny), :] + jnp.where(lane == zc, extra, 0.0)
                xs1[b, side, c] = (1.0 - OMEGA) * v + (gain * force + pull * near)
            y0 = side * (ny - 1)
            at_y = pl.ds(y0, nx, stride=ny)
            gain, pull = coefficients(st[b, at_y, :], cl[b, at_y, :])
            lane = lax.broadcasted_iota(jnp.int32, (nx, depth), 1)
            for c in range(3):
                v = yf[b, side, c]
                inner = u[b, pl.ds(c * cells + y0 + 1 - 2 * side, nx, stride=ny), :]
                near = yh0[b, side, c] + inner + beside_z(v)
                near = near + beside_rows(v, xh0[b, 0, c, y0 : y0 + 1], xh0[b, 1, c, y0 : y0 + 1])
                rows = turned[nx * side : nx * side + nx]
                extra = pltpu.roll(rows, (zc - c * half - y0 % half) % depth, 1)
                force = ld[b, pl.ds(c * cells + y0, nx, stride=ny), :] + jnp.where(lane == zc, extra, 0.0)
                ys1[b, side, c] = (1.0 - OMEGA) * v + (gain * force + pull * near)
        for way, there, dev in ways():
            @pl.when(there)
            def _():
                halo_copy(b, way, dev, lambda b, w: xs1.at[b, w], ys1, xh1, yh1, h1_s, h1_r).start()

    faces(0)
    for d in range(1, n_sub):
        part_arrival(0, d).wait_recv()

    @pl.when(has_prev)
    def _():
        for d in range(n_sub):
            part_arrival(-1, d).wait_recv()

    total = rec[0]
    for o in range(1, targets):
        total = total + rec[o]
    react[1] = -total
    faces(1)

    for d in range(1, n_sub):
        tab_copy(0, d).wait_send()
        part_copy(0, d).wait_send()

    @pl.when(has_prev)
    def _():
        for d in range(n_sub):
            tab_copy(-1, d).wait_send()

    @pl.when(has_next)
    def _():
        for d in range(n_sub):
            part_copy(1, d).wait_send()

    for b in range(2):
        for way, there, dev in ways():
            @pl.when(there)
            def _():
                halo_copy(b, way, dev, x_plane, yf, xh0, yh0, h0_s, h0_r).wait_send()
                halo_copy(b, way, dev, lambda b, w: xs1.at[b, w], ys1, xh1, yh1, h1_s, h1_r).wait_send()
                halo_arrival(b, way, dev, xh1, yh1, h1_s, h1_r).wait_recv()


def relax_kernel(
    nx, ny, chunks,
    disp_c, disp_m, load_c, load_m, stiff_c, stiff_m, clamp_c, clamp_m,
    react, xh0, yh0, xh1, yh1,
    out_c, out_m,
    u, w, ld, st, cl, in_sem, out_sem,
):
    depth = 128
    half = ny // 2
    step = nx // chunks
    sources = ((disp_c, load_c, stiff_c, clamp_c), (disp_m, load_m, stiff_m, clamp_m))
    outs = (out_c, out_m)

    def arrivals(b, k):
        span = pl.ds(k * step, step)
        shifted = pl.ds(k * step + 1, step)
        disp, load, stiff, clamp = sources[b]
        return (
            pltpu.make_async_copy(disp.at[:, span], u.at[b, :, shifted], in_sem.at[b, k, 0]),
            pltpu.make_async_copy(load.at[:, span], ld.at[b, :, span], in_sem.at[b, k, 1]),
            pltpu.make_async_copy(stiff.at[span], st.at[b, span], in_sem.at[b, k, 2]),
            pltpu.make_async_copy(clamp.at[span], cl.at[b, span], in_sem.at[b, k, 3]),
        )

    for b in range(2):
        for k in range(chunks):
            for copy in arrivals(b, k):
                copy.start()

    lane = lax.broadcasted_iota(jnp.int32, (ny, depth), 1)

    def first(b, k):
        zc = (depth - 1, 0)[b]

        def at_x(x, carry):
            gain, pull = coefficients(st[b, x], cl[b, x])
            st[b, x] = pull
            for c in range(3):
                v = u[b, c, x + 1]
                near = u[b, c, x] + u[b, c, x + 2] + beside_z(v)
                near = near + beside_rows(v, yh0[b, 0, c, pl.ds(x, 1)], yh0[b, 1, c, pl.ds(x, 1)])
                rows = react[b, c * half : (c + 1) * half]
                extra = jnp.concatenate(
                    [pltpu.roll(rows, lax.rem(zc - x - nx * h + 2 * depth, depth), 1) for h in range(2)], axis=0)
                push = gain * (ld[b, c, x] + jnp.where(lane == zc, extra, 0.0))
                ld[b, c, x] = push
                w[b, c, x + 1] = (1.0 - OMEGA) * v + (push + pull * near)
            return carry

        lax.fori_loop(k * step, (k + 1) * step, at_x, 0, unroll=2)

    def second(b, k):
        def at_x(x, carry):
            pull = st[b, x]
            for c in range(3):
                v = w[b, c, x + 1]
                near = w[b, c, x] + w[b, c, x + 2] + beside_z(v)
                near = near + beside_rows(v, yh1[b, 0, c, pl.ds(x, 1)], yh1[b, 1, c, pl.ds(x, 1)])
                u[b, c, x + 1] = (1.0 - OMEGA) * v + (ld[b, c, x] + pull * near)
            return carry

        lax.fori_loop(k * step, (k + 1) * step, at_x, 0, unroll=2)

    def departure(b, k):
        return pltpu.make_async_copy(
            u.at[b, :, pl.ds(k * step + 1, step)], outs[b].at[:, pl.ds(k * step, step)], out_sem.at[b, k])

    for b in range(2):
        u[b, :, 0] = xh0[b, 0]
        u[b, :, nx + 1] = xh0[b, 1]
        w[b, :, 0] = xh1[b, 0]
        w[b, :, nx + 1] = xh1[b, 1]
        for copy in arrivals(b, 0):
            copy.wait()
        for k in range(chunks):
            if k + 1 < chunks:
                for copy in arrivals(b, k + 1):
                    copy.wait()
            first(b, k)
            if k >= 1:
                second(b, k - 1)
                departure(b, k - 1).start()
        second(b, chunks - 1)
        departure(b, chunks - 1).start()
    for b in range(2):
        for k in range(chunks):
            departure(b, k).wait()


def on_device(
    n_slab, n_sub,
    cav_disp, cav_load, cav_stiff, cav_clamp, mnt_disp, mnt_load, mnt_stiff, mnt_clamp,
    pair_owner, pair_row, pair_seg, pair_weight, pair_tilt, pair_gap,
):
    nx, ny, depth = cav_stiff.shape
    half = ny // 2
    dense = 3 * half
    targets = 2 * n_sub
    flat = lambda a: a.reshape(-1, depth)
    square = lambda a: a.reshape(-1, 128)
    x_shape = (2, 2, 3, ny, depth)
    y_shape = (2, 2, 3, nx, depth)
    hbm = pl.BlockSpec(memory_space=pl.ANY)
    vmem = pl.BlockSpec(memory_space=pltpu.VMEM)
    dma = pltpu.SemaphoreType.DMA
    shape = lambda dims: jax.ShapeDtypeStruct(dims, F32)
    rows = nx * ny
    halos = pl.pallas_call(
        functools.partial(contact_kernel, n_slab, n_sub, nx, ny),
        out_shape=[shape((2, dense, depth)), shape(x_shape), shape(y_shape), shape(x_shape), shape(y_shape)],
        in_specs=[hbm] * 8 + [vmem] * 6,
        out_specs=[vmem] * 5,
        scratch_shapes=[
            pltpu.VMEM((2, 3 * rows, depth), F32),
            pltpu.VMEM((2, 3 * rows, depth), F32),
            pltpu.VMEM((2, rows, depth), F32),
            pltpu.VMEM((2, rows, depth), jnp.int32),
            pltpu.VMEM((targets, dense, depth), F32),
            pltpu.VMEM((targets, dense, depth), F32),
            pltpu.VMEM((targets, dense, depth), F32),
            pltpu.VMEM(y_shape, F32),
            pltpu.VMEM(x_shape, F32),
            pltpu.VMEM(y_shape, F32),
            dma((targets,)), dma((targets,)), dma((targets,)), dma((targets,)),
            dma((2, 4)), dma((2, 4)), dma((2, 4)), dma((2, 4)), dma((8,)),
        ],
        compiler_params=pltpu.CompilerParams(
            collective_id=0, has_side_effects=True, vmem_limit_bytes=48 * 1024 * 1024),
        name="contact",
    )(
        flat(cav_disp), flat(mnt_disp), flat(cav_load), flat(mnt_load),
        flat(cav_stiff), flat(mnt_stiff), flat(cav_clamp), flat(mnt_clamp),
        square(pair_seg), square(pair_row), square(pair_owner), square(pair_weight), square(pair_gap), pair_tilt,
    )
    chunks = 8
    return tuple(pl.pallas_call(
        functools.partial(relax_kernel, nx, ny, chunks),
        out_shape=[shape(cav_disp.shape), shape(mnt_disp.shape)],
        in_specs=[hbm] * 8 + [vmem] * 5,
        out_specs=[hbm] * 2,
        scratch_shapes=[
            pltpu.VMEM((2, 3, nx + 2, ny, depth), F32),
            pltpu.VMEM((2, 3, nx + 2, ny, depth), F32),
            pltpu.VMEM((2, 3, nx, ny, depth), F32),
            pltpu.VMEM((2, nx, ny, depth), F32),
            pltpu.VMEM((2, nx, ny, depth), jnp.int32),
            dma((2, chunks, 4)), dma((2, chunks)),
        ],
        compiler_params=pltpu.CompilerParams(vmem_limit_bytes=48 * 1024 * 1024),
        name="relax",
    )(
        cav_disp, mnt_disp, cav_load, mnt_load, cav_stiff, mnt_stiff, cav_clamp, mnt_clamp, *halos
    ))


def solution(mesh):
    field = P(None, "slab", "sub", None)
    cells = P("slab", "sub", None)
    both = P(("slab", "sub"))
    return jax.shard_map(
        functools.partial(on_device, mesh.shape["slab"], mesh.shape["sub"]),
        mesh=mesh,
        in_specs=(
            field, field, cells, cells, field, field, cells, cells,
            P(("slab", "sub"), None), both, both, both, P(None, ("slab", "sub")), both,
        ),
        out_specs=(field, field),
        check_vma=False,
    )
```

profile of v0, /device:TPU:4, one launch (start us, length us, event | category | flops | bytes accessed | tf_op | source)
XLA Modules:
  0.0 61.8 jit_solution(15181296683479463029)
XLA Ops:
  0.6 0.0 copy-start
  0.6 1.2 %copy-done = f32[64,32,128]{2,1,0:T(8,128)S(1)} copy-done((f32[64,32,128]{2,1,0:T(8,128)S(1)}, f32[64,32,128]{2,1,0:T(8,128)}, u32[]{:S(2)}) %copy-start) | copy-done | bytes 1048600
  1.9 0.0 copy-start.1
  1.9 1.2 %copy-done.1 = f32[64,32,128]{2,1,0:T(8,128)S(1)} copy-done((f32[64,32,128]{2,1,0:T(8,128)S(1)}, f32[64,32,128]{2,1,0:T(8,128)}, u32[]{:S(2)}) %copy-start.1) | copy-done | bytes 1048600
  3.1 0.0 copy-start.2
  3.1 1.2 %copy-done.2 = s32[64,32,128]{2,1,0:T(8,128)S(1)} copy-done((s32[64,32,128]{2,1,0:T(8,128)S(1)}, s32[64,32,128]{2,1,0:T(8,128)}, u32[]{:S(2)}) %copy-start.2) | copy-done | bytes 1048600
  4.3 0.0 copy-start.3
  4.3 1.2 %copy-done.3 = s32[64,32,128]{2,1,0:T(8,128)S(1)} copy-done((s32[64,32,128]{2,1,0:T(8,128)S(1)}, s32[64,32,128]{2,1,0:T(8,128)}, u32[]{:S(2)}) %copy-start.3) | copy-done | bytes 1048600
  5.5 0.0 copy-start.4
  5.5 0.7 %copy-done.4 = f32[2,2048]{1,0:T(2,128)S(1)} copy-done((f32[2,2048]{1,0:T(2,128)S(1)}, f32[2,2048]{1,0:T(2,128)}, u32[]{:S(2)}) %copy-start.4) | copy-done | bytes 16408
  6.3 0.0 copy-start.5
  6.3 0.7 %copy-done.5 = s32[2048]{0:T(1024)S(1)} copy-done((s32[2048]{0:T(1024)S(1)}, s32[2048]{0:T(1024)}, u32[]{:S(2)}) %copy-start.5) | copy-done | bytes 8216
  7.0 0.0 copy-start.6
  7.0 0.7 %copy-done.6 = s32[2048]{0:T(1024)S(1)} copy-done((s32[2048]{0:T(1024)S(1)}, s32[2048]{0:T(1024)}, u32[]{:S(2)}) %copy-start.6) | copy-done | bytes 8216
  7.6 0.0 copy-start.7
  7.7 0.7 %copy-done.7 = s32[2048,1]{0,1:T(1,128)S(1)} copy-done((s32[2048,1]{0,1:T(1,128)S(1)}, s32[2048,1]{0,1:T(1,128)}, u32[]{:S(2)}) %copy-start.7) | copy-done | bytes 8216
  8.3 0.0 copy-start.8
  8.3 0.7 %copy-done.8 = f32[2048]{0:T(1024)S(1)} copy-done((f32[2048]{0:T(1024)S(1)}, f32[2048]{0:T(1024)}, u32[]{:S(2)}) %copy-start.8) | copy-done | bytes 8216
  9.0 0.0 copy-start.9
  9.0 0.7 %copy-done.9 = f32[2048]{0:T(1024)S(1)} copy-done((f32[2048]{0:T(1024)S(1)}, f32[2048]{0:T(1024)}, u32[]{:S(2)}) %copy-start.9) | copy-done | bytes 8216
  9.7 27.4 %contact.1 = (f32[2,48,128]{2,1,0:T(8,128)S(1)}, f32[2,2,3,32,128]{4,3,2,1,0:T(8,128)S(1)}, f32[2,2,3,64,128]{4,3,2,1,0:T(8,128)S(1)}, f32[2,2,3,32,128]{4,3,2,1,0:T(8,128)S(1)}, f32[2,2,3,64,128]{4,3,2,1,0:T(8,128)S(1)}) custom-call(f32[6144,128]{1,0:T(8,128)} %bitcast.22, f32[6144,128]{1,0:T(8,128)} %bitcast.23, f32[6144,128]{1,0:T(8,128)} %bitcast.24, ...), custom_call_target="tpu_custom_call" | custom-call | tf_op jit(solution)/shard_map/contact/pallas_call | solution.py:477
  37.1 24.7 %relax.1 = (f32[3,64,32,128]{3,2,1,0:T(8,128)}, f32[3,64,32,128]{3,2,1,0:T(8,128)}) custom-call(f32[3,64,32,128]{3,2,1,0:T(8,128)} %disp_c.1, f32[3,64,32,128]{3,2,1,0:T(8,128)} %disp_m.1, f32[3,64,32,128]{3,2,1,0:T(8,128)} %load_c.1, f32[3,64,32,128]{3,2,1,0:T(8,128)} %load_m.1, f32[64,32,128]{2,1,0:T(8,128)S(1)} %copy-done, f32[64,32,128]{2,1,0:T(8,128)S(1)} %copy-done.1, ...), custom_call_target="tpu_custom_call" | custom-call | tf_op jit(solution)/shard_map/relax/pallas_call | solution.py:505
Async XLA Ops:
  0.6 1.2 %copy-start = (f32[64,32,128]{2,1,0:T(8,128)S(1)}, f32[64,32,128]{2,1,0:T(8,128)}, u32[]{:S(2)}) copy-start(f32[64,32,128]{2,1,0:T(8,128)} %stiff_c.1) | copy-start | bytes 3145732
  1.9 1.2 %copy-start.1 = (f32[64,32,128]{2,1,0:T(8,128)S(1)}, f32[64,32,128]{2,1,0:T(8,128)}, u32[]{:S(2)}) copy-start(f32[64,32,128]{2,1,0:T(8,128)} %stiff_m.1) | copy-start | bytes 3145732
  3.1 1.2 %copy-start.2 = (s32[64,32,128]{2,1,0:T(8,128)S(1)}, s32[64,32,128]{2,1,0:T(8,128)}, u32[]{:S(2)}) copy-start(s32[64,32,128]{2,1,0:T(8,128)} %clamp_c.1) | copy-start | bytes 3145732
  4.3 1.2 %copy-start.3 = (s32[64,32,128]{2,1,0:T(8,128)S(1)}, s32[64,32,128]{2,1,0:T(8,128)}, u32[]{:S(2)}) copy-start(s32[64,32,128]{2,1,0:T(8,128)} %clamp_m.1) | copy-start | bytes 3145732
  5.5 0.7 %copy-start.4 = (f32[2,2048]{1,0:T(2,128)S(1)}, f32[2,2048]{1,0:T(2,128)}, u32[]{:S(2)}) copy-start(f32[2,2048]{1,0:T(2,128)} %tilt.1) | copy-start | bytes 49156
  6.3 0.7 %copy-start.5 = (s32[2048]{0:T(1024)S(1)}, s32[2048]{0:T(1024)}, u32[]{:S(2)}) copy-start(s32[2048]{0:T(1024)} %param.24) | copy-start | bytes 24580
  7.0 0.7 %copy-start.6 = (s32[2048]{0:T(1024)S(1)}, s32[2048]{0:T(1024)}, u32[]{:S(2)}) copy-start(s32[2048]{0:T(1024)} %param.23) | copy-start | bytes 24580
  7.6 0.7 %copy-start.7 = (s32[2048,1]{0,1:T(1,128)S(1)}, s32[2048,1]{0,1:T(1,128)}, u32[]{:S(2)}) copy-start(s32[2048,1]{0,1:T(1,128)} %param.22) | copy-start | bytes 24580
  8.3 0.7 %copy-start.8 = (f32[2048]{0:T(1024)S(1)}, f32[2048]{0:T(1024)}, u32[]{:S(2)}) copy-start(f32[2048]{0:T(1024)} %param.25) | copy-start | bytes 24580
  9.0 0.7 %copy-start.9 = (f32[2048]{0:T(1024)S(1)}, f32[2048]{0:T(1024)}, u32[]{:S(2)}) copy-start(f32[2048]{0:T(1024)} %param.27) | copy-start | bytes 24580
where the time goes:
time: 62.4 us; the launch traced here: 61.8 us
  Pallas kernels  52.1 us (83%)
  local copies, waits for them, and re-layouts  9.09 us (15%)
  between operations  0.66 us (1%)
    pallas_call x1, Pallas kernels, on_device(): pl.pallas_call(functools.partial(contact_kernel, n_slab, n_sub, nx, ny),...  27.4 us
    pallas_call x1, Pallas kernels, on_device(): pl.pallas_call(functools.partial(relax_kernel, nx, ny, chunks), out_shape...  24.7 us
    unnamed x20, local copies, waits for them, and re-layouts  9.09 us

commit v1 on v0

--- a/solution.py
+++ b/solution.py
@@ -48,8 +48,9 @@
 def contact_kernel(
     n_slab, n_sub, nx, ny,
     disp_c, disp_m, load_c, load_m, stiff_c, stiff_m, clamp_c, clamp_m,
+    seg_in, row_in, own_in, weight_in, gap0_in, tilt_in,
+    react, xh0, yh0, xh1, yh1,
     seg, row, own, weight, gap0, tilt,
-    react, xh0, yh0, xh1, yh1,
     u, ld, st, cl, tab, part, rec, yf, xs1, ys1,
     tab_s, tab_r, part_s, part_r, h0_s, h0_r, h1_s, h1_r, in_sem,
 ):
@@ -67,6 +68,7 @@
     loads = []
     for i, (src, dst) in enumerate((
         (disp_m, u.at[1]), (disp_c, u.at[0]),
+        (seg_in, seg), (row_in, row), (own_in, own), (weight_in, weight), (gap0_in, gap0), (tilt_in, tilt),
         (stiff_m, st.at[1]), (clamp_m, cl.at[1]), (load_m, ld.at[1]),
         (stiff_c, st.at[0]), (clamp_c, cl.at[0]), (load_c, ld.at[0]),
     )):
@@ -198,6 +200,8 @@
         for d in range(n_sub):
             tab_arrival(1, d).wait_recv()
 
+    for copy in loads[2:8]:
+        copy.wait()
     targets = 2 * n_sub
     table = tab[...].reshape(targets * dense, depth)
     tab_parts = jnp.concatenate([v.astype(BF16) for v in split3(table)], axis=1)
@@ -283,7 +287,7 @@
     def _():
         rec[pl.ds(n_sub, n_sub)] = jnp.zeros((n_sub, dense, depth), F32)
 
-    for copy in loads[2:]:
+    for copy in loads[8:]:
         copy.wait()
     for b in range(2):
         for way, there, dev in ways():
@@ -416,7 +420,7 @@
                 w[b, c, x + 1] = (1.0 - OMEGA) * v + (push + pull * near)
             return carry
 
-        lax.fori_loop(k * step, (k + 1) * step, at_x, 0, unroll=2)
+        lax.fori_loop(0, step, lambda i, carry: at_x(k * step + i, carry), 0, unroll=True)
 
     def second(b, k):
         def at_x(x, carry):
@@ -428,7 +432,7 @@
                 u[b, c, x + 1] = (1.0 - OMEGA) * v + (ld[b, c, x] + pull * near)
             return carry
 
-        lax.fori_loop(k * step, (k + 1) * step, at_x, 0, unroll=2)
+        lax.fori_loop(0, step, lambda i, carry: at_x(k * step + i, carry), 0, unroll=True)
 
     def departure(b, k):
         return pltpu.make_async_copy(
@@ -441,14 +445,23 @@
         w[b, :, nx + 1] = xh1[b, 1]
         for copy in arrivals(b, 0):
             copy.wait()
-        for k in range(chunks):
-            if k + 1 < chunks:
+
+        def chunk(k, carry, b=b):
+            @pl.when(k + 1 < chunks)
+            def _():
                 for copy in arrivals(b, k + 1):
                     copy.wait()
+
             first(b, k)
-            if k >= 1:
+
+            @pl.when(k >= 1)
+            def _():
                 second(b, k - 1)
                 departure(b, k - 1).start()
+
+            return carry
+
+        lax.fori_loop(0, chunks, chunk, 0)
         second(b, chunks - 1)
         departure(b, chunks - 1).start()
     for b in range(2):
@@ -469,17 +482,20 @@
     square = lambda a: a.reshape(-1, 128)
     x_shape = (2, 2, 3, ny, depth)
     y_shape = (2, 2, 3, nx, depth)
-    hbm = pl.BlockSpec(memory_space=pl.ANY)
+    hbm = pl.BlockSpec(memory_space=pltpu.HBM)
     vmem = pl.BlockSpec(memory_space=pltpu.VMEM)
     dma = pltpu.SemaphoreType.DMA
     shape = lambda dims: jax.ShapeDtypeStruct(dims, F32)
     rows = nx * ny
+    pairs = pair_row.shape[0]
     halos = pl.pallas_call(
         functools.partial(contact_kernel, n_slab, n_sub, nx, ny),
         out_shape=[shape((2, dense, depth)), shape(x_shape), shape(y_shape), shape(x_shape), shape(y_shape)],
-        in_specs=[hbm] * 8 + [vmem] * 6,
+        in_specs=[hbm] * 14,
         out_specs=[vmem] * 5,
         scratch_shapes=[
+            *[pltpu.VMEM((pairs // 128, 128), kind) for kind in (jnp.int32,) * 3 + (F32,) * 2],
+            pltpu.VMEM((2, pairs), F32),
             pltpu.VMEM((2, 3 * rows, depth), F32),
             pltpu.VMEM((2, 3 * rows, depth), F32),
             pltpu.VMEM((2, rows, depth), F32),
@@ -491,10 +507,10 @@
             pltpu.VMEM(x_shape, F32),
             pltpu.VMEM(y_shape, F32),
             dma((targets,)), dma((targets,)), dma((targets,)), dma((targets,)),
-            dma((2, 4)), dma((2, 4)), dma((2, 4)), dma((2, 4)), dma((8,)),
+            dma((2, 4)), dma((2, 4)), dma((2, 4)), dma((2, 4)), dma((14,)),
         ],
         compiler_params=pltpu.CompilerParams(
-            collective_id=0, has_side_effects=True, vmem_limit_bytes=48 * 1024 * 1024),
+            collective_id=0, has_side_effects=True, vmem_limit_bytes=65_500 * 1024),
         name="contact",
     )(
         flat(cav_disp), flat(mnt_disp), flat(cav_load), flat(mnt_load),
@@ -515,7 +531,7 @@
             pltpu.VMEM((2, nx, ny, depth), jnp.int32),
             dma((2, chunks, 4)), dma((2, chunks)),
         ],
-        compiler_params=pltpu.CompilerParams(vmem_limit_bytes=48 * 1024 * 1024),
+        compiler_params=pltpu.CompilerParams(vmem_limit_bytes=65_500 * 1024),
         name="relax",
     )(
         cav_disp, mnt_disp, cav_load, mnt_load, cav_stiff, mnt_stiff, cav_clamp, mnt_clamp, *halos

time: 62.4 us -> 44.1 us (0.71)
  the two profiles are of different devices: /device:TPU:4 before, /device:TPU:1 now
where the time goes in v1:
time: 44.1 us; the launch traced here: 43.4 us
  Pallas kernels  42.7 us (97%)
  between operations  0.64 us (1%)
    pallas_call x1, Pallas kernels, on_device(): pl.pallas_call(functools.partial(contact_kernel, n_slab, n_sub, nx, ny),...  27.8 us
    pallas_call x1, Pallas kernels, on_device(): pl.pallas_call(functools.partial(relax_kernel, nx, ny, chunks), out_shape...  15 us

profile of v1, /device:TPU:1, one launch (start us, length us, event | category | flops | bytes accessed | tf_op | source)
XLA Modules:
  0.0 43.4 jit_solution(13323218527634097859)
XLA Ops:
  0.6 27.8 %contact.1 = (f32[2,48,128]{2,1,0:T(8,128)}, f32[2,2,3,32,128]{4,3,2,1,0:T(8,128)}, f32[2,2,3,64,128]{4,3,2,1,0:T(8,128)}, f32[2,2,3,32,128]{4,3,2,1,0:T(8,128)}, f32[2,2,3,64,128]{4,3,2,1,0:T(8,128)}) custom-call(f32[6144,128]{1,0:T(8,128)} %bitcast.13, f32[6144,128]{1,0:T(8,128)} %bitcast.14, f32[6144,128]{1,0:T(8,128)} %bitcast.15, f32[6144,128]{1,0:T(8,128)} %bitcast.16, ...), custom_call_target="tpu_custom_call" | custom-call | tf_op jit(solution)/shard_map/contact/pallas_call | solution.py:491
  28.4 15.0 %relax.1 = (f32[3,64,32,128]{3,2,1,0:T(8,128)}, f32[3,64,32,128]{3,2,1,0:T(8,128)}) custom-call(f32[3,64,32,128]{3,2,1,0:T(8,128)} %disp_c.1, f32[3,64,32,128]{3,2,1,0:T(8,128)} %disp_m.1, f32[3,64,32,128]{3,2,1,0:T(8,128)} %load_c.1, f32[3,64,32,128]{3,2,1,0:T(8,128)} %load_m.1, f32[64,32,128]{2,1,0:T(8,128)} %stiff_c.1, f32[64,32,128]{2,1,0:T(8,128)} %stiff_m.1, ...), custom_call_target="tpu_custom_call" | custom-call | tf_op jit(solution)/shard_map/relax/pallas_call | solution.py:521

commit v2 on v1

--- a/solution.py
+++ b/solution.py
@@ -14,6 +14,7 @@
 F32 = jnp.float32
 BF16 = jnp.bfloat16
 CHUNK = 256
+CHUNKS = 8
 
 
 def split3(v):
@@ -49,10 +50,10 @@
     n_slab, n_sub, nx, ny,
     disp_c, disp_m, load_c, load_m, stiff_c, stiff_m, clamp_c, clamp_m,
     seg_in, row_in, own_in, weight_in, gap0_in, tilt_in,
-    react, xh0, yh0, xh1, yh1,
-    seg, row, own, weight, gap0, tilt,
+    w_out, push_out, pull_out, xh1, yh1,
+    react, xh0, yh0, w, seg, row, own, weight, gap0, tilt,
     u, ld, st, cl, tab, part, rec, yf, xs1, ys1,
-    tab_s, tab_r, part_s, part_r, h0_s, h0_r, h1_s, h1_r, in_sem,
+    tab_s, tab_r, part_s, part_r, h0_s, h0_r, h1_s, h1_r, in_sem, out_sem,
 ):
     s = lax.axis_index("slab")
     t = lax.axis_index("sub")
@@ -67,7 +68,7 @@
 
     loads = []
     for i, (src, dst) in enumerate((
-        (disp_m, u.at[1]), (disp_c, u.at[0]),
+        (disp_m, u.at[1, :, pl.ds(ny, cells)]), (disp_c, u.at[0, :, pl.ds(ny, cells)]),
         (seg_in, seg), (row_in, row), (own_in, own), (weight_in, weight), (gap0_in, gap0), (tilt_in, tilt),
         (stiff_m, st.at[1]), (clamp_m, cl.at[1]), (load_m, ld.at[1]),
         (stiff_c, st.at[0]), (clamp_c, cl.at[0]), (load_c, ld.at[0]),
@@ -102,8 +103,8 @@
             for c in range(3):
                 for h in range(2):
                     want = x + nx * h
-                    start = pl.multiple_of(c * cells + x * ny + half * h, 8)
-                    tile = u[b, pl.ds(start, half), :]
+                    start = pl.multiple_of(ny + x * ny + half * h, 8)
+                    tile = u[b, c, pl.ds(start, half), :]
                     moved = pltpu.roll(tile, lax.rem(want - zc + depth, depth), 1)
                     acc[c] = jnp.where(lane == want, moved, acc[c])
             return tuple(acc)
@@ -115,7 +116,7 @@
     tab[t] = densify(1)
     for b, side in ((1, 0), (1, 1)):
         for c in range(3):
-            yf[b, side, c] = u[b, pl.ds(c * cells + side * (ny - 1), nx, stride=ny), :]
+            yf[b, side, c] = u[b, c, pl.ds(ny + side * (ny - 1), nx, stride=ny), :]
 
     sides = has_prev.astype(jnp.int32) + has_next.astype(jnp.int32)
     pl.semaphore_wait(barrier, n_sub - 1 + n_sub * sides)
@@ -167,7 +168,7 @@
         return remote(dst, dst, ss.at[b, way], rs.at[b, way], dev)
 
     def x_plane(b, way):
-        return u.at[b].reshape(3, nx, ny, depth).at[:, (nx - 1) * way]
+        return u.at[b, :, pl.ds(ny + (nx - 1) * ny * way, ny)]
 
     def start_halo0(b):
         for way, there, dev in ways():
@@ -187,7 +188,7 @@
     loads[1].wait()
     for side in range(2):
         for c in range(3):
-            yf[0, side, c] = u[0, pl.ds(c * cells + side * (ny - 1), nx, stride=ny), :]
+            yf[0, side, c] = u[0, c, pl.ds(ny + side * (ny - 1), nx, stride=ny), :]
     start_halo0(0)
     cav_dense = densify(0)
     cav_parts = jnp.concatenate([v.astype(BF16) for v in split3(cav_dense)], axis=1)
@@ -306,14 +307,14 @@
             gain, pull = coefficients(st[b, at_x, :], cl[b, at_x, :])
             lane = lax.broadcasted_iota(jnp.int32, (ny, depth), 1)
             for c in range(3):
-                v = u[b, pl.ds(c * cells + x0 * ny, ny), :]
-                inner = u[b, pl.ds(c * cells + (x0 + 1 - 2 * side) * ny, ny), :]
+                v = u[b, c, pl.ds(ny + x0 * ny, ny), :]
+                inner = u[b, c, pl.ds(ny + (x0 + 1 - 2 * side) * ny, ny), :]
                 near = xh0[b, side, c] + inner + beside_z(v)
                 near = near + beside_rows(v, yh0[b, 0, c, x0 : x0 + 1], yh0[b, 1, c, x0 : x0 + 1])
                 rows = force_b[c * half : (c + 1) * half]
                 extra = jnp.concatenate(
                     [pltpu.roll(rows, (zc - x0 - nx * h) % depth, 1) for h in range(2)], axis=0)
-                force = ld[b, pl.ds(c * cells + x0 * ny, ny), :] + jnp.where(lane == zc, extra, 0.0)
+                force = ld[b, c, pl.ds(x0 * ny, ny), :] + jnp.where(lane == zc, extra, 0.0)
                 xs1[b, side, c] = (1.0 - OMEGA) * v + (gain * force + pull * near)
             y0 = side * (ny - 1)
             at_y = pl.ds(y0, nx, stride=ny)
@@ -321,19 +322,58 @@
             lane = lax.broadcasted_iota(jnp.int32, (nx, depth), 1)
             for c in range(3):
                 v = yf[b, side, c]
-                inner = u[b, pl.ds(c * cells + y0 + 1 - 2 * side, nx, stride=ny), :]
+                inner = u[b, c, pl.ds(ny + y0 + 1 - 2 * side, nx, stride=ny), :]
                 near = yh0[b, side, c] + inner + beside_z(v)
                 near = near + beside_rows(v, xh0[b, 0, c, y0 : y0 + 1], xh0[b, 1, c, y0 : y0 + 1])
                 rows = turned[nx * side : nx * side + nx]
                 extra = pltpu.roll(rows, (zc - c * half - y0 % half) % depth, 1)
-                force = ld[b, pl.ds(c * cells + y0, nx, stride=ny), :] + jnp.where(lane == zc, extra, 0.0)
+                force = ld[b, c, pl.ds(y0, nx, stride=ny), :] + jnp.where(lane == zc, extra, 0.0)
                 ys1[b, side, c] = (1.0 - OMEGA) * v + (gain * force + pull * near)
         for way, there, dev in ways():
             @pl.when(there)
             def _():
                 halo_copy(b, way, dev, lambda b, w: xs1.at[b, w], ys1, xh1, yh1, h1_s, h1_r).start()
 
+    planes = nx // CHUNKS
+    zone = lax.broadcasted_iota(jnp.int32, (ny, depth), 1)
+
+    def leaving(b, k):
+        span = pl.ds(pl.multiple_of(k * planes * ny, 8), planes * ny)
+        return (
+            pltpu.make_async_copy(w.at[b, :, span], w_out.at[b, :, span], out_sem.at[b, k, 0]),
+            pltpu.make_async_copy(ld.at[b, :, span], push_out.at[b, :, span], out_sem.at[b, k, 1]),
+            pltpu.make_async_copy(st.at[b, span], pull_out.at[b, span], out_sem.at[b, k, 2]),
+        )
+
+    def first(b):
+        zc = lane_of[b]
+        u[b, :, pl.ds(0, ny)] = xh0[b, 0]
+        u[b, :, pl.ds(ny + cells, ny)] = xh0[b, 1]
+
+        def chunk(k, carry):
+            for i in range(planes):
+                x = k * planes + i
+                at = [pl.ds(pl.multiple_of((x + j) * ny, 8), ny) for j in range(3)]
+                gain, pull = coefficients(st[b, at[0], :], cl[b, at[0], :])
+                st[b, at[0], :] = pull
+                for c in range(3):
+                    v = u[b, c, at[1], :]
+                    near = u[b, c, at[0], :] + u[b, c, at[2], :] + beside_z(v)
+                    near = near + beside_rows(v, yh0[b, 0, c, pl.ds(x, 1)], yh0[b, 1, c, pl.ds(x, 1)])
+                    rows = react[b, c * half : (c + 1) * half]
+                    extra = jnp.concatenate(
+                        [pltpu.roll(rows, lax.rem(zc - x - nx * h + 2 * depth, depth), 1) for h in range(2)], axis=0)
+                    push = gain * (ld[b, c, at[0], :] + jnp.where(zone == zc, extra, 0.0))
+                    ld[b, c, at[0], :] = push
+                    w[b, c, at[0], :] = (1.0 - OMEGA) * v + (push + pull * near)
+            for copy in leaving(b, k):
+                copy.start()
+            return carry
+
+        lax.fori_loop(0, CHUNKS, chunk, 0)
+
     faces(0)
+    first(0)
     for d in range(1, n_sub):
         part_arrival(0, d).wait_recv()
 
@@ -347,6 +387,7 @@
         total = total + rec[o]
     react[1] = -total
     faces(1)
+    first(1)
 
     for d in range(1, n_sub):
         tab_copy(0, d).wait_send()
@@ -369,103 +410,61 @@
                 halo_copy(b, way, dev, x_plane, yf, xh0, yh0, h0_s, h0_r).wait_send()
                 halo_copy(b, way, dev, lambda b, w: xs1.at[b, w], ys1, xh1, yh1, h1_s, h1_r).wait_send()
                 halo_arrival(b, way, dev, xh1, yh1, h1_s, h1_r).wait_recv()
+    for b in range(2):
+        for k in range(CHUNKS):
+            for copy in leaving(b, k):
+                copy.wait()
 
 
 def relax_kernel(
-    nx, ny, chunks,
-    disp_c, disp_m, load_c, load_m, stiff_c, stiff_m, clamp_c, clamp_m,
-    react, xh0, yh0, xh1, yh1,
-    out_c, out_m,
-    u, w, ld, st, cl, in_sem, out_sem,
+    nx, ny, w_in, push_in, pull_in, xh1, yh1, out_c, out_m, u, w, ld, st, in_sem, out_sem
 ):
-    depth = 128
-    half = ny // 2
-    step = nx // chunks
-    sources = ((disp_c, load_c, stiff_c, clamp_c), (disp_m, load_m, stiff_m, clamp_m))
+    step = nx // CHUNKS
     outs = (out_c, out_m)
 
     def arrivals(b, k):
         span = pl.ds(k * step, step)
-        shifted = pl.ds(k * step + 1, step)
-        disp, load, stiff, clamp = sources[b]
         return (
-            pltpu.make_async_copy(disp.at[:, span], u.at[b, :, shifted], in_sem.at[b, k, 0]),
-            pltpu.make_async_copy(load.at[:, span], ld.at[b, :, span], in_sem.at[b, k, 1]),
-            pltpu.make_async_copy(stiff.at[span], st.at[b, span], in_sem.at[b, k, 2]),
-            pltpu.make_async_copy(clamp.at[span], cl.at[b, span], in_sem.at[b, k, 3]),
+            pltpu.make_async_copy(w_in.at[b, :, span], w.at[b, :, pl.ds(k * step + 1, step)], in_sem.at[b, k, 0]),
+            pltpu.make_async_copy(push_in.at[b, :, span], ld.at[b, :, span], in_sem.at[b, k, 1]),
+            pltpu.make_async_copy(pull_in.at[b, span], st.at[b, span], in_sem.at[b, k, 2]),
         )
 
+    def departure(b, k):
+        span = pl.ds(k * step, step)
+        return pltpu.make_async_copy(u.at[b, :, span], outs[b].at[:, span], out_sem.at[b, k])
+
     for b in range(2):
-        for k in range(chunks):
+        for k in range(CHUNKS):
             for copy in arrivals(b, k):
                 copy.start()
 
-    lane = lax.broadcasted_iota(jnp.int32, (ny, depth), 1)
-
-    def first(b, k):
-        zc = (depth - 1, 0)[b]
-
-        def at_x(x, carry):
-            gain, pull = coefficients(st[b, x], cl[b, x])
-            st[b, x] = pull
-            for c in range(3):
-                v = u[b, c, x + 1]
-                near = u[b, c, x] + u[b, c, x + 2] + beside_z(v)
-                near = near + beside_rows(v, yh0[b, 0, c, pl.ds(x, 1)], yh0[b, 1, c, pl.ds(x, 1)])
-                rows = react[b, c * half : (c + 1) * half]
-                extra = jnp.concatenate(
-                    [pltpu.roll(rows, lax.rem(zc - x - nx * h + 2 * depth, depth), 1) for h in range(2)], axis=0)
-                push = gain * (ld[b, c, x] + jnp.where(lane == zc, extra, 0.0))
-                ld[b, c, x] = push
-                w[b, c, x + 1] = (1.0 - OMEGA) * v + (push + pull * near)
-            return carry
-
-        lax.fori_loop(0, step, lambda i, carry: at_x(k * step + i, carry), 0, unroll=True)
-
-    def second(b, k):
-        def at_x(x, carry):
-            pull = st[b, x]
-            for c in range(3):
-                v = w[b, c, x + 1]
-                near = w[b, c, x] + w[b, c, x + 2] + beside_z(v)
-                near = near + beside_rows(v, yh1[b, 0, c, pl.ds(x, 1)], yh1[b, 1, c, pl.ds(x, 1)])
-                u[b, c, x + 1] = (1.0 - OMEGA) * v + (ld[b, c, x] + pull * near)
-            return carry
-
-        lax.fori_loop(0, step, lambda i, carry: at_x(k * step + i, carry), 0, unroll=True)
-
-    def departure(b, k):
-        return pltpu.make_async_copy(
-            u.at[b, :, pl.ds(k * step + 1, step)], outs[b].at[:, pl.ds(k * step, step)], out_sem.at[b, k])
-
     for b in range(2):
-        u[b, :, 0] = xh0[b, 0]
-        u[b, :, nx + 1] = xh0[b, 1]
         w[b, :, 0] = xh1[b, 0]
         w[b, :, nx + 1] = xh1[b, 1]
         for copy in arrivals(b, 0):
             copy.wait()
 
         def chunk(k, carry, b=b):
-            @pl.when(k + 1 < chunks)
+            @pl.when(k + 1 < CHUNKS)
             def _():
                 for copy in arrivals(b, k + 1):
                     copy.wait()
 
-            first(b, k)
-
-            @pl.when(k >= 1)
-            def _():
-                second(b, k - 1)
-                departure(b, k - 1).start()
-
+            for i in range(step):
+                x = k * step + i
+                pull = st[b, x]
+                for c in range(3):
+                    v = w[b, c, x + 1]
+                    near = w[b, c, x] + w[b, c, x + 2] + beside_z(v)
+                    near = near + beside_rows(v, yh1[b, 0, c, pl.ds(x, 1)], yh1[b, 1, c, pl.ds(x, 1)])
+                    u[b, c, x] = (1.0 - OMEGA) * v + (ld[b, c, x] + pull * near)
+            departure(b, k).start()
             return carry
 
-        lax.fori_loop(0, chunks, chunk, 0)
-        second(b, chunks - 1)
-        departure(b, chunks - 1).start()
+        lax.fori_loop(0, CHUNKS, chunk, 0)
     for b in range(2):
-        for k in range(chunks):
+        for k in range(CHUNKS):
             departure(b, k).wait()
 
 
@@ -478,7 +477,7 @@
     half = ny // 2
     dense = 3 * half
     targets = 2 * n_sub
-    flat = lambda a: a.reshape(-1, depth)
+    flat = lambda a: a.reshape(*a.shape[:-3], -1, depth)
     square = lambda a: a.reshape(-1, 128)
     x_shape = (2, 2, 3, ny, depth)
     y_shape = (2, 2, 3, nx, depth)
@@ -490,14 +489,17 @@
     pairs = pair_row.shape[0]
     halos = pl.pallas_call(
         functools.partial(contact_kernel, n_slab, n_sub, nx, ny),
-        out_shape=[shape((2, dense, depth)), shape(x_shape), shape(y_shape), shape(x_shape), shape(y_shape)],
+        out_shape=[
+            shape((2, 3, rows, depth)), shape((2, 3, rows, depth)), shape((2, rows, depth)), shape(x_shape), shape(y_shape)],
         in_specs=[hbm] * 14,
-        out_specs=[vmem] * 5,
+        out_specs=[hbm] * 3 + [vmem] * 2,
         scratch_shapes=[
+            pltpu.VMEM((2, dense, depth), F32), pltpu.VMEM(x_shape, F32), pltpu.VMEM(y_shape, F32),
+            pltpu.VMEM((2, 3, rows, depth), F32),
             *[pltpu.VMEM((pairs // 128, 128), kind) for kind in (jnp.int32,) * 3 + (F32,) * 2],
             pltpu.VMEM((2, pairs), F32),
-            pltpu.VMEM((2, 3 * rows, depth), F32),
-            pltpu.VMEM((2, 3 * rows, depth), F32),
+            pltpu.VMEM((2, 3, rows + 2 * ny, depth), F32),
+            pltpu.VMEM((2, 3, rows, depth), F32),
             pltpu.VMEM((2, rows, depth), F32),
             pltpu.VMEM((2, rows, depth), jnp.int32),
             pltpu.VMEM((targets, dense, depth), F32),
@@ -507,7 +509,7 @@
             pltpu.VMEM(x_shape, F32),
             pltpu.VMEM(y_shape, F32),
             dma((targets,)), dma((targets,)), dma((targets,)), dma((targets,)),
-            dma((2, 4)), dma((2, 4)), dma((2, 4)), dma((2, 4)), dma((14,)),
+            dma((2, 4)), dma((2, 4)), dma((2, 4)), dma((2, 4)), dma((14,)), dma((2, CHUNKS, 3)),
         ],
         compiler_params=pltpu.CompilerParams(
             collective_id=0, has_side_effects=True, vmem_limit_bytes=65_500 * 1024),
@@ -517,25 +519,23 @@
         flat(cav_stiff), flat(mnt_stiff), flat(cav_clamp), flat(mnt_clamp),
         square(pair_seg), square(pair_row), square(pair_owner), square(pair_weight), square(pair_gap), pair_tilt,
     )
-    chunks = 8
+    w, push, pull, xh1, yh1 = halos
+    solid = lambda a: a.reshape(*a.shape[:-2], nx, ny, depth)
     return tuple(pl.pallas_call(
-        functools.partial(relax_kernel, nx, ny, chunks),
+        functools.partial(relax_kernel, nx, ny),
         out_shape=[shape(cav_disp.shape), shape(mnt_disp.shape)],
-        in_specs=[hbm] * 8 + [vmem] * 5,
+        in_specs=[hbm] * 3 + [vmem] * 2,
         out_specs=[hbm] * 2,
         scratch_shapes=[
-            pltpu.VMEM((2, 3, nx + 2, ny, depth), F32),
+            pltpu.VMEM((2, 3, nx, ny, depth), F32),
             pltpu.VMEM((2, 3, nx + 2, ny, depth), F32),
             pltpu.VMEM((2, 3, nx, ny, depth), F32),
             pltpu.VMEM((2, nx, ny, depth), F32),
-            pltpu.VMEM((2, nx, ny, depth), jnp.int32),
-            dma((2, chunks, 4)), dma((2, chunks)),
+            dma((2, CHUNKS, 3)), dma((2, CHUNKS)),
         ],
         compiler_params=pltpu.CompilerParams(vmem_limit_bytes=65_500 * 1024),
         name="relax",
-    )(
-        cav_disp, mnt_disp, cav_load, mnt_load, cav_stiff, mnt_stiff, cav_clamp, mnt_clamp, *halos
-    ))
+    )(solid(w), solid(push), solid(pull), xh1, yh1))
 
 
 def solution(mesh):

time: 44.1 us -> 39.9 us (0.905); the launches traced: 43.4 us -> 39.7 us
  Pallas kernels: 42.7 us -> 39.1 us
    pallas_call x1, Pallas kernels: 15 us -> 9.69 us  [on_device(): pl.pallas_call(functools.partial(relax_kernel, nx, ny), out_shape=[shape(...]
    pallas_call x1, Pallas kernels: 27.8 us -> 29.4 us  [on_device(): pl.pallas_call(functools.partial(contact_kernel, n_slab, n_sub, nx, ny),...]
where the time goes in v2:
time: 39.9 us; the launch traced here: 39.7 us
  Pallas kernels  39.1 us (98%)
  between operations  0.64 us (2%)
    pallas_call x1, Pallas kernels, on_device(): pl.pallas_call(functools.partial(contact_kernel, n_slab, n_sub, nx, ny),...  29.4 us
    pallas_call x1, Pallas kernels, on_device(): pl.pallas_call(functools.partial(relax_kernel, nx, ny), out_shape=[shape(...  9.69 us

profile of v2, /device:TPU:1, one launch (start us, length us, event | category | flops | bytes accessed | tf_op | source)
XLA Modules:
  0.0 39.7 jit_solution(7939650091103871987)
XLA Ops:
  0.6 29.4 %contact.1 = (f32[2,3,2048,128]{3,2,1,0:T(8,128)}, f32[2,3,2048,128]{3,2,1,0:T(8,128)}, f32[2,2048,128]{2,1,0:T(8,128)}, f32[2,2,3,32,128]{4,3,2,1,0:T(8,128)}, f32[2,2,3,64,128]{4,3,2,1,0:T(8,128)}) custom-call(f32[3,2048,128]{2,1,0:T(8,128)} %bitcast.18, f32[3,2048,128]{2,1,0:T(8,128)} %bitcast.19, f32[3,2048,128]{2,1,0:T(8,128)} %bitcast.20, ...), custom_call_target="tpu_custom_call" | custom-call | tf_op jit(solution)/shard_map/contact/pallas_call | solution.py:490
  30.0 9.7 %relax.1 = (f32[3,64,32,128]{3,2,1,0:T(8,128)}, f32[3,64,32,128]{3,2,1,0:T(8,128)}) custom-call(f32[2,3,64,32,128]{4,3,2,1,0:T(8,128)} %bitcast.16, f32[2,3,64,32,128]{4,3,2,1,0:T(8,128)} %bitcast.17, f32[2,64,32,128]{3,2,1,0:T(8,128)} %bitcast.22, f32[2,2,3,32,128]{4,3,2,1,0:T(8,128)} %get-tuple-element.10.xh1, f32[2,2,3,64,128]{4,3,2,1,0:T(8,128)} %get-tuple-element.11.yh1), custom_call_target="tpu_custom_call" | custom-call | tf_op jit(solution)/shard_map/relax/pallas_call | solution.py:524

commit v3 on v2

--- a/solution.py
+++ b/solution.py
@@ -17,11 +17,9 @@
 CHUNKS = 8
 
 
-def split3(v):
+def split2(v):
     hi = v.astype(BF16).astype(F32)
-    rest = v - hi
-    mid = rest.astype(BF16).astype(F32)
-    return hi, mid, rest - mid
+    return hi, v - hi
 
 
 def beside_z(v):
@@ -66,6 +64,23 @@
     has_next = s < n_slab - 1
     lane_of = (depth - 1, 0)
 
+    def peer(ds, d):
+        return {"slab": s + ds, "sub": lax.rem(t + d, n_sub)}
+
+    barrier = pltpu.get_barrier_semaphore()
+    for d in range(1, n_sub):
+        pl.semaphore_signal(barrier, inc=1, device_id=peer(0, d), device_id_type=MESH)
+
+    @pl.when(has_prev)
+    def _():
+        for d in range(n_sub):
+            pl.semaphore_signal(barrier, inc=1, device_id=peer(-1, d), device_id_type=MESH)
+
+    @pl.when(has_next)
+    def _():
+        for d in range(n_sub):
+            pl.semaphore_signal(barrier, inc=1, device_id=peer(1, d), device_id_type=MESH)
+
     loads = []
     for i, (src, dst) in enumerate((
         (disp_m, u.at[1, :, pl.ds(ny, cells)]), (disp_c, u.at[0, :, pl.ds(ny, cells)]),
@@ -77,23 +92,6 @@
         copy.start()
         loads.append(copy)
 
-    def peer(ds, d):
-        return {"slab": s + ds, "sub": lax.rem(t + d, n_sub)}
-
-    barrier = pltpu.get_barrier_semaphore()
-    for d in range(1, n_sub):
-        pl.semaphore_signal(barrier, inc=1, device_id=peer(0, d), device_id_type=MESH)
-
-    @pl.when(has_prev)
-    def _():
-        for d in range(n_sub):
-            pl.semaphore_signal(barrier, inc=1, device_id=peer(-1, d), device_id_type=MESH)
-
-    @pl.when(has_next)
-    def _():
-        for d in range(n_sub):
-            pl.semaphore_signal(barrier, inc=1, device_id=peer(1, d), device_id_type=MESH)
-
     def densify(b):
         zc = lane_of[b]
         lane = lax.broadcasted_iota(jnp.int32, (half, depth), 1)
@@ -110,7 +108,7 @@
             return tuple(acc)
 
         zero = jnp.zeros((half, depth), F32)
-        return jnp.concatenate(lax.fori_loop(0, nx, at_x, (zero,) * 3, unroll=4), axis=0)
+        return jnp.concatenate(lax.fori_loop(0, nx, at_x, (zero,) * 3, unroll=8), axis=0)
 
     loads[0].wait()
     tab[t] = densify(1)
@@ -191,7 +189,7 @@
             yf[0, side, c] = u[0, c, pl.ds(ny + side * (ny - 1), nx, stride=ny), :]
     start_halo0(0)
     cav_dense = densify(0)
-    cav_parts = jnp.concatenate([v.astype(BF16) for v in split3(cav_dense)], axis=1)
+    cav_parts = jnp.concatenate([v.astype(BF16) for v in split2(cav_dense)], axis=1)
 
     for d in range(1, n_sub):
         tab_arrival(0, d).wait_recv()
@@ -205,7 +203,7 @@
         copy.wait()
     targets = 2 * n_sub
     table = tab[...].reshape(targets * dense, depth)
-    tab_parts = jnp.concatenate([v.astype(BF16) for v in split3(table)], axis=1)
+    tab_parts = jnp.concatenate([v.astype(BF16) for v in split2(table)], axis=1)
 
     def line(ref, k):
         per = CHUNK // 128
@@ -229,8 +227,8 @@
         hot_c = (lane_id == lanes(row_k)).astype(F32).astype(BF16)
         mask_m = key_id == target * half + seg_k % half
         mask_c = small_id == row_k % half
-        rows_m = dot(tab_parts, jnp.concatenate([hot_m] * 3, axis=0), (((1,), (0,)), ((), ())))
-        rows_c = dot(cav_parts, jnp.concatenate([hot_c] * 3, axis=0), (((1,), (0,)), ((), ())))
+        rows_m = dot(tab_parts, jnp.concatenate([hot_m] * 2, axis=0), (((1,), (0,)), ((), ())))
+        rows_c = dot(cav_parts, jnp.concatenate([hot_c] * 2, axis=0), (((1,), (0,)), ((), ())))
         sl_a = tilt[0:1, k * CHUNK : (k + 1) * CHUNK]
         sl_b = tilt[1:2, k * CHUNK : (k + 1) * CHUNK]
         scale = 1.0 / jnp.sqrt(1.0 + sl_a * sl_a + sl_b * sl_b)
@@ -248,9 +246,9 @@
         z = -BETA * gap
         soft = jnp.maximum(z, 0.0) + jnp.log1p(jnp.exp(-jnp.abs(z)))
         press = line(weight, k) * (KNORM * soft / BETA)
-        push = [split3(press * normal[c]) for c in range(3)]
+        push = [split2(press * normal[c]) for c in range(3)]
         left_m, left_c = [], []
-        for p in range(3):
+        for p in range(2):
             left_m.append(jnp.concatenate(
                 [
                     jnp.where(mask_m[o * half : (o + 1) * half], push[c][p], 0.0)
@@ -259,9 +257,9 @@
             left_c.append(jnp.concatenate(
                 [jnp.where(mask_c, push[c][p], 0.0) for c in range(3)], axis=0).astype(BF16))
         mnt_sum = mnt_sum + dot(
-            jnp.concatenate(left_m, axis=1), jnp.concatenate([hot_m] * 3, axis=1), (((1,), (1,)), ((), ())))
+            jnp.concatenate(left_m, axis=1), jnp.concatenate([hot_m] * 2, axis=1), (((1,), (1,)), ((), ())))
         cav_sum = cav_sum + dot(
-            jnp.concatenate(left_c, axis=1), jnp.concatenate([hot_c] * 3, axis=1), (((1,), (1,)), ((), ())))
+            jnp.concatenate(left_c, axis=1), jnp.concatenate([hot_c] * 2, axis=1), (((1,), (1,)), ((), ())))
     part[...] = mnt_sum.reshape(targets, dense, depth)
     react[0] = cav_sum
 

time: 39.9 us -> 38.5 us (0.965)
  Pallas kernels: 39.1 us -> 37.7 us
    pallas_call x1, Pallas kernels: 29.4 us -> 28 us  [on_device(): pl.pallas_call(functools.partial(contact_kernel, n_slab, n_sub, nx, ny),...]
where the time goes in v3:
time: 38.5 us; the launch traced here: 38.4 us
  Pallas kernels  37.7 us (98%)
  between operations  0.64 us (2%)
    pallas_call x1, Pallas kernels, on_device(): pl.pallas_call(functools.partial(contact_kernel, n_slab, n_sub, nx, ny),...  28 us
    pallas_call x1, Pallas kernels, on_device(): pl.pallas_call(functools.partial(relax_kernel, nx, ny), out_shape=[shape(...  9.69 us

profile of v3, /device:TPU:1, one launch (start us, length us, event | category | flops | bytes accessed | tf_op | source)
XLA Modules:
  0.0 38.4 jit_solution(2283435738816343368)
XLA Ops:
  0.6 28.0 %contact.1 = (f32[2,3,2048,128]{3,2,1,0:T(8,128)}, f32[2,3,2048,128]{3,2,1,0:T(8,128)}, f32[2,2048,128]{2,1,0:T(8,128)}, f32[2,2,3,32,128]{4,3,2,1,0:T(8,128)}, f32[2,2,3,64,128]{4,3,2,1,0:T(8,128)}) custom-call(f32[3,2048,128]{2,1,0:T(8,128)} %bitcast.18, f32[3,2048,128]{2,1,0:T(8,128)} %bitcast.19, f32[3,2048,128]{2,1,0:T(8,128)} %bitcast.20, ...), custom_call_target="tpu_custom_call" | custom-call | tf_op jit(solution)/shard_map/contact/pallas_call | solution.py:488
  28.7 9.7 %relax.1 = (f32[3,64,32,128]{3,2,1,0:T(8,128)}, f32[3,64,32,128]{3,2,1,0:T(8,128)}) custom-call(f32[2,3,64,32,128]{4,3,2,1,0:T(8,128)} %bitcast.16, f32[2,3,64,32,128]{4,3,2,1,0:T(8,128)} %bitcast.17, f32[2,64,32,128]{3,2,1,0:T(8,128)} %bitcast.22, f32[2,2,3,32,128]{4,3,2,1,0:T(8,128)} %get-tuple-element.10.xh1, f32[2,2,3,64,128]{4,3,2,1,0:T(8,128)} %get-tuple-element.11.yh1), custom_call_target="tpu_custom_call" | custom-call | tf_op jit(solution)/shard_map/relax/pallas_call | solution.py:522
